TPU v7x, 32 devices: a whole 2x2x4 slice. The times are simulated.
32 devices in a mesh: ctx: 32 (over z, y, x, core), hid: 1.
Axes of the slice: x: 2, y: 2, z: 4, core: 2. Of those that a mesh axis runs over, the one named last changes fastest.
Arguments:
- queries: bfloat16 [8192, 4096], P('ctx', 'hid'), may hold values from -8 to 8
- keys: bfloat16 [8192, 1024], P('ctx', 'hid'), may hold values from -5 to 5
- values: bfloat16 [8192, 1024], P('ctx', 'hid'), may hold values from -6 to 6
- residual: bfloat16 [8192, 4096], P('ctx', 'hid'), may hold values from -6 to 6
- out_weight: bfloat16 [4096, 4096], P('hid'), may hold values from -0.09375 to 0.09375
Outputs:
- layer_out: bfloat16 [8192, 4096], P('ctx', 'hid')
All inputs are finite; a program needn't handle non-finite values.
Results may differ from a plain program's by a relative error of at most 0.0044.
Values may be sent and summed in bfloat16 or wider, within the bound.
A program may use at most 128 MiB of HBM per device.

v0:
```python
import math

import jax
import jax.numpy as jnp
from jax import lax
from jax.sharding import PartitionSpec as P

HEAD_SIZE = 128


def passed_along(block, axis, distance):
    devices = range(lax.axis_size(axis))
    route = [(i - distance, i) for i in devices if i - distance in devices]
    return lax.ppermute(block, axis, route)


def block_mask(local_rows, position):
    row_ids = lax.broadcasted_iota(jnp.int32, (local_rows, 5 * local_rows), 0)
    col_ids = lax.broadcasted_iota(jnp.int32, (local_rows, 5 * local_rows), 1)
    block_ids = col_ids // local_rows
    offset = col_ids - block_ids * local_rows
    distance = jnp.where(
        block_ids == 0, 0, jnp.left_shift(jnp.int32(1), jnp.maximum(block_ids - 1, 0))
    )
    return jnp.where(block_ids == 0, offset <= row_ids, position >= distance)


def attend(queries, gathered_rows, position):
    local_rows = queries.shape[0]
    kv_heads = gathered_rows.shape[2] // HEAD_SIZE
    queries_per_group = queries.shape[1] // HEAD_SIZE // kv_heads
    reshaped_output = queries.reshape(local_rows, kv_heads, queries_per_group, HEAD_SIZE)
    key_matrix = gathered_rows[0].reshape(-1, kv_heads, HEAD_SIZE)
    value_matrix = gathered_rows[1].reshape(-1, kv_heads, HEAD_SIZE)
    scores = jnp.einsum(
        "qkgd,skd->kgqs", reshaped_output, key_matrix, preferred_element_type=jnp.float32
    ) / math.sqrt(HEAD_SIZE)
    scores = jnp.where(block_mask(local_rows, position), scores, -1e30)
    row_peak = jnp.max(scores, axis=-1, keepdims=True)
    raised = jnp.exp(scores - row_peak)
    weights = (raised / jnp.sum(raised, axis=-1, keepdims=True)).astype(jnp.bfloat16)
    mixed = jnp.einsum("kgqs,skd->qkgd", weights, value_matrix, preferred_element_type=jnp.float32)
    return mixed.reshape(local_rows, -1).astype(jnp.bfloat16)


def on_device(queries, keys, values, residual, out_weight):
    position = lax.axis_index("ctx")
    stacked = jnp.stack([keys, values])
    pieces = []
    for distance in (1, 2, 4, 8):
        pieces.append(passed_along(stacked, "ctx", distance))
    gathered_rows = jnp.concatenate([stacked] + pieces, axis=1)
    attended = attend(queries, gathered_rows, position)
    summed = lax.psum_scatter(
        lax.dot_general(
            out_weight, attended, (((0,), (1,)), ((), ())), preferred_element_type=jnp.float32
        ).astype(jnp.bfloat16),
        "hid",
        scatter_dimension=0,
        tiled=True,
    ).astype(jnp.float32)
    return (residual.astype(jnp.float32) + summed.T).astype(jnp.bfloat16)


def solution(mesh):
    return jax.shard_map(
        on_device,
        mesh=mesh,
        in_specs=(
            P("ctx", "hid"),
            P("ctx", "hid"),
            P("ctx", "hid"),
            P("ctx", "hid"),
            P("hid", None),
        ),
        out_specs=P("ctx", "hid"),
        check_vma=False,
    )
```

profile of v0, /device:TPU:15, one launch (start us, length us, event | category | flops | bytes accessed | tf_op | source)
XLA Modules:
  0.0 160.7 jit_solution(17739046822032021002)
XLA Ops:
  0.0 0.0 copy-start
  0.0 1.4 copy.9
  1.4 1.2 copy.10
  2.6 1.6 %pad_maximum_fusion = (bf16[2,256,1024]{1,2,0:T(8,128)(2,1)}, bf16[2,1280,1024]{1,2,0:T(8,128)(2,1)}) fusion(bf16[1,256,1024]{1,2,0:T(8,128)(2,1)S(1)} %bitcast.30, bf16[1,256,1024]{1,2,0:T(8,128)(2,1)S(1)} %bitcast.29), kind=kLoop, calls=%fused_computation.28 | loop fusion | flops 2097151 | bytes 3145728 | tf_op jit(solution)/shard_map/stack | solution.py:48
  4.3 3.7 %collective-permute-start = (bf16[2,256,1024]{1,2,0:T(8,128)(2,1)}, bf16[2,256,1024]{1,2,0:T(8,128)(2,1)}, u32[]{:S(2)}, u32[]{:S(2)}) collective-permute-start(bf16[2,256,1024]{1,2,0:T(8,128)(2,1)} %get-tuple-element.7), channel_id=1, source_target_pairs={{0,1},{1,2},{2,3},{3,4},{4,5},{5,6},{6,7},{7,8},{8,9},{9,10},{10,1... | collective-permute-start | bytes 3145736 | tf_op jit(solution)/shard_map/ppermute | solution.py:14
  8.0 3.1 %collective-permute-start.1 = (bf16[2,256,1024]{1,2,0:T(8,128)(2,1)}, bf16[2,256,1024]{1,2,0:T(8,128)(2,1)}, u32[]{:S(2)}, u32[]{:S(2)}) collective-permute-start(bf16[2,256,1024]{1,2,0:T(8,128)(2,1)} %get-tuple-element.7), channel_id=1, source_target_pairs={{0,2},{1,3},{2,4},{3,5},{4,6},{5,7},{6,8},{7,9},{8,10},{9,11},{10,... | collective-permute-start | bytes 3145736 | tf_op jit(solution)/shard_map/ppermute | solution.py:14
  11.1 3.1 %collective-permute-start.2 = (bf16[2,256,1024]{1,2,0:T(8,128)(2,1)}, bf16[2,256,1024]{1,2,0:T(8,128)(2,1)}, u32[]{:S(2)}, u32[]{:S(2)}) collective-permute-start(bf16[2,256,1024]{1,2,0:T(8,128)(2,1)} %get-tuple-element.7), channel_id=1, source_target_pairs={{0,4},{1,5},{2,6},{3,7},{4,8},{5,9},{6,10},{7,11},{8,12},{9,13},{1... | collective-permute-start | bytes 3145736 | tf_op jit(solution)/shard_map/ppermute | solution.py:14
  14.2 3.2 %collective-permute-start.3 = (bf16[2,256,1024]{1,2,0:T(8,128)(2,1)}, bf16[2,256,1024]{1,2,0:T(8,128)(2,1)S(1)}, u32[]{:S(2)}, u32[]{:S(2)}) collective-permute-start(bf16[2,256,1024]{1,2,0:T(8,128)(2,1)} %get-tuple-element.7), channel_id=1, source_target_pairs={{0,8},{1,9},{2,10},{3,11},{4,12},{5,13},{6,14},{7,15},{8,16},{9,17... | collective-permute-start | bytes 3145736 | tf_op jit(solution)/shard_map/ppermute | solution.py:14
  17.5 0.0 copy-done
  17.5 2.7 %reshape.7 = bf16[256,8,4,128]{3,2,1,0:T(4,128)(2,1)} reshape(bf16[256,4096]{1,0:T(8,128)(2,1)S(1)} %copy-done) | data formatting | bytes 4194304 | tf_op jit(solution)/shard_map/reshape | solution.py:32
  20.2 1.1 fusion.18
  21.3 17.9 %collective-permute-done = bf16[2,256,1024]{1,2,0:T(8,128)(2,1)} collective-permute-done((bf16[2,256,1024]{1,2,0:T(8,128)(2,1)}, bf16[2,256,1024]{1,2,0:T(8,128)(2,1)}, u32[]{:S(2)}, u32[]{:S(2)}) %collective-permute-start) | collective-permute-done | bytes 1048608 | tf_op jit(solution)/shard_map/ppermute | solution.py:14
  39.2 2.3 %constant_dynamic-update-slice_fusion.3 = bf16[2,1280,1024]{1,2,0:T(8,128)(2,1)} fusion(bf16[2,1280,1024]{1,2,0:T(8,128)(2,1)} %get-tuple-element.8, bf16[2,256,1024]{1,2,0:T(8,128)(2,1)} %collective-permute-done), kind=kLoop, calls=%fused_computation.35 | loop fusion | bytes 2097152
  41.5 24.3 %collective-permute-done.1 = bf16[2,256,1024]{1,2,0:T(8,128)(2,1)} collective-permute-done((bf16[2,256,1024]{1,2,0:T(8,128)(2,1)}, bf16[2,256,1024]{1,2,0:T(8,128)(2,1)}, u32[]{:S(2)}, u32[]{:S(2)}) %collective-permute-start.1) | collective-permute-done | bytes 1048608 | tf_op jit(solution)/shard_map/ppermute | solution.py:14
  65.8 2.3 %constant_dynamic-update-slice_fusion.2 = bf16[2,1280,1024]{1,2,0:T(8,128)(2,1)} fusion(bf16[2,1280,1024]{1,2,0:T(8,128)(2,1)} %constant_dynamic-update-slice_fusion.3, bf16[2,256,1024]{1,2,0:T(8,128)(2,1)} %collective-permute-done.1), kind=kLoop, calls=%fused_computation.34 | loop fusion | bytes 2097152
  68.1 20.1 %collective-permute-done.2 = bf16[2,256,1024]{1,2,0:T(8,128)(2,1)} collective-permute-done((bf16[2,256,1024]{1,2,0:T(8,128)(2,1)}, bf16[2,256,1024]{1,2,0:T(8,128)(2,1)}, u32[]{:S(2)}, u32[]{:S(2)}) %collective-permute-start.2) | collective-permute-done | bytes 1048608 | tf_op jit(solution)/shard_map/ppermute | solution.py:14
  88.3 2.3 %constant_dynamic-update-slice_fusion.1 = bf16[2,1280,1024]{1,2,0:T(8,128)(2,1)} fusion(bf16[2,1280,1024]{1,2,0:T(8,128)(2,1)} %constant_dynamic-update-slice_fusion.2, bf16[2,256,1024]{1,2,0:T(8,128)(2,1)} %collective-permute-done.2), kind=kLoop, calls=%fused_computation.33 | loop fusion | bytes 2097152
  90.6 12.0 %collective-permute-done.3 = bf16[2,256,1024]{1,2,0:T(8,128)(2,1)S(1)} collective-permute-done((bf16[2,256,1024]{1,2,0:T(8,128)(2,1)}, bf16[2,256,1024]{1,2,0:T(8,128)(2,1)S(1)}, u32[]{:S(2)}, u32[]{:S(2)}) %collective-permute-start.3) | collective-permute-done | bytes 1048608 | tf_op jit(solution)/shard_map/ppermute | solution.py:14
  102.6 1.2 constant_dynamic-update-slice_fusion
  103.7 4.4 %fusion.30 = (bf16[1,1280,1024]{1,2,0:T(8,128)(2,1)S(1)}, bf16[1,1280,1024]{1,2,0:T(8,128)(2,1)}) fusion(bf16[2,1280,1024]{1,2,0:T(8,128)(2,1)} %constant_dynamic-update-slice_fusion), kind=kLoop, calls=%fused_computation.43 | loop fusion | bytes 10485760 | tf_op jit(solution)/shard_map/slice | solution.py:33
  108.1 19.6 %fusion.31 = (f32[8,4,256]{2,1,0:T(4,128)S(1)}, f32[8,4,256,1280]{2,3,1,0:T(8,128)}) fusion(pred[256,1280]{0,1:T(8,128)(4,1)S(1)} %fusion.18, bf16[1280,8,128,1]{0,2,3,1:T(8,128)(2,1)S(1)} %bitcast.28, bf16[256,8,4,128]{3,2,1,0:T(4,128)(2,1)} %reshape.7), kind=kOutput, calls=%fused_computation.44 | convolution fusion | flops 2726298880 | bytes 47022080 | tf_op jit(solution)/shard_map/sub | solution.py:40
  127.7 15.4 %fusion.11 = bf16[8,128,4,256]{3,1,2,0:T(8,128)(2,1)S(1)} fusion(bf16[1280,8,128,1]{0,2,3,1:T(8,128)(2,1)} %bitcast.27, f32[8,4,256,1280]{2,3,1,0:T(8,128)} %get-tuple-element.10, f32[8,4,256]{2,1,0:T(4,128)S(1)} %get-tuple-element.9), kind=kOutput, calls=%fused_computation.17 | convolution fusion | flops 2706374656 | bytes 46694400 | tf_op jit(solution)/shard_map/kgqs,skd->qkgd/dot_general | solution.py:42
  143.1 17.5 %fusion.8 = bf16[256,4096]{1,0:T(8,128)(2,1)} fusion(bf16[256,4096]{0,1:T(8,128)(2,1)S(1)} %bitcast.26, bf16[4096,4096]{1,0:T(8,128)(2,1)} %param.9, bf16[256,4096]{1,0:T(8,128)(2,1)} %param.8), kind=kOutput, calls=%fused_computation.12 | convolution fusion | flops 8595177472 | bytes 39845888 | tf_op jit(solution)/shard_map/dot_general | solution.py:55
  (2 shorter events, 0.0 us)
Async XLA Ops:
  0.0 17.5 %copy-start = (bf16[256,4096]{1,0:T(8,128)(2,1)S(1)}, bf16[256,4096]{1,0:T(8,128)(2,1)}, u32[]{:S(2)}) copy-start(bf16[256,4096]{1,0:T(8,128)(2,1)} %param.5) | copy-start | bytes 6291460
  4.3 34.9 %collective-permute-start = (bf16[2,256,1024]{1,2,0:T(8,128)(2,1)}, bf16[2,256,1024]{1,2,0:T(8,128)(2,1)}, u32[]{:S(2)}, u32[]{:S(2)}) collective-permute-start(bf16[2,256,1024]{1,2,0:T(8,128)(2,1)} %get-tuple-element.7), channel_id=1, source_target_pairs={{0,1},{1,2},{2,3},{3,4},{4,5},{5,6},{6,7},{7,8},{8,9},{9,10},{10,1... | collective-permute-start | bytes 3145736 | tf_op jit(solution)/shard_map/ppermute | solution.py:14
  8.0 57.8 %collective-permute-start.1 = (bf16[2,256,1024]{1,2,0:T(8,128)(2,1)}, bf16[2,256,1024]{1,2,0:T(8,128)(2,1)}, u32[]{:S(2)}, u32[]{:S(2)}) collective-permute-start(bf16[2,256,1024]{1,2,0:T(8,128)(2,1)} %get-tuple-element.7), channel_id=1, source_target_pairs={{0,2},{1,3},{2,4},{3,5},{4,6},{5,7},{6,8},{7,9},{8,10},{9,11},{10,... | collective-permute-start | bytes 3145736 | tf_op jit(solution)/shard_map/ppermute | solution.py:14
  11.1 77.2 %collective-permute-start.2 = (bf16[2,256,1024]{1,2,0:T(8,128)(2,1)}, bf16[2,256,1024]{1,2,0:T(8,128)(2,1)}, u32[]{:S(2)}, u32[]{:S(2)}) collective-permute-start(bf16[2,256,1024]{1,2,0:T(8,128)(2,1)} %get-tuple-element.7), channel_id=1, source_target_pairs={{0,4},{1,5},{2,6},{3,7},{4,8},{5,9},{6,10},{7,11},{8,12},{9,13},{1... | collective-permute-start | bytes 3145736 | tf_op jit(solution)/shard_map/ppermute | solution.py:14
  14.2 88.3 %collective-permute-start.3 = (bf16[2,256,1024]{1,2,0:T(8,128)(2,1)}, bf16[2,256,1024]{1,2,0:T(8,128)(2,1)S(1)}, u32[]{:S(2)}, u32[]{:S(2)}) collective-permute-start(bf16[2,256,1024]{1,2,0:T(8,128)(2,1)} %get-tuple-element.7), channel_id=1, source_target_pairs={{0,8},{1,9},{2,10},{3,11},{4,12},{5,13},{6,14},{7,15},{8,16},{9,17... | collective-permute-start | bytes 3145736 | tf_op jit(solution)/shard_map/ppermute | solution.py:14
where the time goes:
time: 161 us
  waiting for transfers between devices  74.3 us (46%)
  matrix products  52.5 us (33%)
  local copies, waits for them, and re-layouts  17.9 us (11%)
  starting transfers between devices  13.1 us (8%)
  other arithmetic  2.7 us (2%)
    ppermute x4, waiting for transfers between devices, passed_along(): return lax.ppermute(block, axis, route)  74.3 us
    sub x1, matrix products, attend(): raised = jnp.exp(scores - row_peak)  19.6 us
    dot_general x1, matrix products, on_device(): lax.dot_general(out_weight, attended, (((0,), (1,)), ((), ())), preferred...  17.5 us
    dot_general x1, matrix products, attend(): jnp.einsum('kgqs,skd->qkgd', weights, value_matrix, preferred_element_typ...  15.4 us
    ppermute x4, starting transfers between devices, passed_along(): return lax.ppermute(block, axis, route)  13.1 us
    unnamed x7, local copies, waits for them, and re-layouts  9.62 us
    slice x1, local copies, waits for them, and re-layouts, attend(): key_matrix = gathered_rows[0].reshape(-1, kv_heads, HEAD_SIZE)  4.38 us
  transfers between devices with their start and end apart: 4, of which 4 were waited for; matrix products, arithmetic and copies ran while one was open for 7% of the time, Pallas kernels for 0%

commit v1 on v0

v1 whole, which is shorter than its diff:
```python
import functools
import math

import jax
import jax.numpy as jnp
from jax import lax
from jax.experimental import pallas as pl
from jax.experimental.pallas import tpu as pltpu
from jax.sharding import PartitionSpec as P

HEAD_SIZE = 128
DISTANCES = (8, 4, 2, 1)
SLOT = {8: 4, 4: 3, 2: 2, 1: 1}
MESH = pl.DeviceIdType.MESH
FAR = 1e30


def block_kernel(
    n,
    with_residual,
    q_hbm,
    k_hbm,
    v_hbm,
    res_hbm,
    w_hbm,
    out_hbm,
    kv,
    q_vm,
    w_vm,
    res_vm,
    acc,
    out_vm,
    att,
    own_sem,
    q_sem,
    w_sem,
    res_sem,
    out_sem,
    send_sem,
    recv_sem,
):
    heads = q_vm.shape[0]
    rows = q_vm.shape[1]
    group = q_vm.shape[2] // HEAD_SIZE
    width = acc.shape[1]
    chunks = 2 * heads
    me = lax.axis_index("ctx")

    def own_copy(c):
        source = k_hbm if c % 2 == 0 else v_hbm
        return pltpu.make_async_copy(
            source.at[:, pl.ds((c // 2) * HEAD_SIZE, HEAD_SIZE)],
            kv.at[c, pl.ds(0, rows), :],
            own_sem.at[c],
        )

    def q_copy(h):
        return pltpu.make_async_copy(
            q_hbm.at[:, pl.ds(h * group * HEAD_SIZE, group * HEAD_SIZE)],
            q_vm.at[h],
            q_sem.at[h],
        )

    def w_copy(h):
        depth = group * HEAD_SIZE
        return pltpu.make_async_copy(
            w_hbm.at[pl.ds(h * depth, depth), :], w_vm.at[h], w_sem.at[h]
        )

    for c in range(chunks):
        own_copy(c).start()
    for h in range(heads):
        q_copy(h).start()
    if with_residual:
        res_copy = pltpu.make_async_copy(res_hbm, res_vm, res_sem)
        res_copy.start()
    for h in range(heads):
        w_copy(h).start()

    def bit(distance):
        return (me // distance) % 2

    def partner(distance):
        return me + distance * (1 - 2 * bit(distance))

    barrier = pltpu.get_barrier_semaphore()
    for distance in (4, 2, 1):
        pl.semaphore_signal(
            barrier, inc=1, device_id={"ctx": partner(distance)}, device_id_type=MESH
        )

    for peer in ((me + 8) % n, (me + n - 8) % n):
        pl.semaphore_signal(barrier, inc=1, device_id={"ctx": peer}, device_id_type=MESH)
    pl.semaphore_wait(barrier, 5)

    def send(c, distance, source, target):
        return pltpu.make_async_remote_copy(
            src_ref=kv.at[c, pl.ds(source * rows, rows), :],
            dst_ref=kv.at[c, pl.ds(SLOT[distance] * rows, rows), :],
            send_sem=send_sem.at[SLOT[distance] - 1, c],
            recv_sem=recv_sem.at[SLOT[distance] - 1, c],
            device_id={"ctx": target},
            device_id_type=MESH,
        )

    def sends_own(distance):
        return (me + 8 < n) if distance == 8 else (bit(distance) == 0)

    def sends_on(distance):
        return (bit(distance) == 1) & (me >= 2 * distance)

    for c in range(chunks):
        own_copy(c).wait()
        for distance in DISTANCES:
            @pl.when(sends_own(distance))
            def _():
                target = me + 8 if distance == 8 else partner(distance)
                send(c, distance, 0, target).start()

    for distance in DISTANCES:
        @pl.when(me < distance)
        def _():
            @pl.loop(0, chunks)
            def _(c):
                kv[c, pl.ds(SLOT[distance] * rows, rows), :] = jnp.zeros(
                    (rows, HEAD_SIZE), kv.dtype
                )

    if with_residual:
        res_copy.wait()
        acc[...] = res_vm[...].astype(jnp.float32)
    else:
        acc[...] = jnp.zeros_like(acc)

    def receive(c, distance):
        @pl.when(me >= distance)
        def _():
            send(c, distance, 0, me).wait_recv()

        if distance > 1:
            lower = distance // 2
            @pl.when(sends_on(lower))
            def _():
                send(c, lower, SLOT[distance], partner(lower)).start()

    def turn(t):
        for lag, distance in enumerate(DISTANCES):
            @pl.when((t >= lag) & (t < chunks + lag))
            def _():
                receive(t - lag, distance)

    unit = math.log2(math.e) / math.sqrt(HEAD_SIZE)
    away = {d: jnp.where(me >= d, 0.0, FAR) for d in DISTANCES}

    def attend(h, which):
        key = kv[2 * h]
        value = kv[2 * h + 1]
        value = jnp.concatenate([value, jnp.ones_like(value)], axis=1)
        row = lax.broadcasted_iota(jnp.int32, (rows, rows), 0)
        col = lax.broadcasted_iota(jnp.int32, (rows, rows), 1)
        all_scores = [
            lax.dot_general(
                q_vm[h, :, j * HEAD_SIZE : (j + 1) * HEAD_SIZE],
                key,
                (((1,), (1,)), ((), ())),
                preferred_element_type=jnp.float32,
            )
            for j in which
        ]
        for j, scores in zip(which, all_scores):
            own = jnp.where(col <= row, scores[:, :rows], -FAR)
            peak = jnp.max(own, axis=1, keepdims=True)
            parts = {0: own}
            for d in DISTANCES:
                at = SLOT[d]
                parts[at] = scores[:, at * rows : (at + 1) * rows]
                peak = jnp.maximum(
                    peak, jnp.max(parts[at], axis=1, keepdims=True) - away[d]
                )
            peak = peak * unit
            raised = [jnp.exp2(parts[0] * unit - peak).astype(jnp.bfloat16)]
            for d in reversed(DISTANCES):
                raised.append(
                    jnp.exp2(parts[SLOT[d]] * unit - (peak + away[d])).astype(jnp.bfloat16)
                )
            raised = jnp.concatenate(raised, axis=1)
            mixed = jnp.dot(raised, value, preferred_element_type=jnp.float32)
            mixed = mixed[:, :HEAD_SIZE] / mixed[:, HEAD_SIZE:]
            att[:, j * HEAD_SIZE : (j + 1) * HEAD_SIZE] = mixed.astype(jnp.bfloat16)

    lead = 2
    half = group // 2

    @pl.loop(0, heads + lead)
    def _(i):
        h = i - lead
        turn(2 * i)

        @pl.when(h >= 0)
        def _():
            q_copy(h).wait()
            attend(h, range(half))

        turn(2 * i + 1)

        @pl.when(h >= 0)
        def _():
            attend(h, range(half, group))
            w_copy(h).wait()
            step = min(1024, width)
            for at in range(0, width, step):
                acc[:, at : at + step] += jnp.dot(
                    att[...],
                    w_vm[h, :, at : at + step],
                    preferred_element_type=jnp.float32,
                )

    out_vm[...] = acc[...].astype(out_vm.dtype)
    out_copy = pltpu.make_async_copy(out_vm, out_hbm, out_sem)
    out_copy.start()

    for distance in DISTANCES:
        sent = sends_own(distance)
        if distance < 8:
            sent = sent | sends_on(distance)

        @pl.when(sent)
        def _():
            @pl.loop(0, chunks)
            def _(c):
                send(c, distance, 0, me).wait_send()

    out_copy.wait()


def on_device(n, hid, queries, keys, values, residual, out_weight):
    rows, columns = queries.shape
    heads = keys.shape[1] // HEAD_SIZE
    width = out_weight.shape[1]
    group_columns = columns // heads
    chunks = 2 * heads
    with_residual = hid == 1
    out_type = jnp.bfloat16 if with_residual else jnp.float32
    result = pl.pallas_call(
        functools.partial(block_kernel, n, with_residual),
        out_shape=jax.ShapeDtypeStruct((rows, width), out_type),
        in_specs=[pl.BlockSpec(memory_space=pl.ANY)] * 5,
        out_specs=pl.BlockSpec(memory_space=pl.ANY),
        scratch_shapes=[
            pltpu.VMEM((chunks, 5 * rows, HEAD_SIZE), jnp.bfloat16),
            pltpu.VMEM((heads, rows, group_columns), jnp.bfloat16),
            pltpu.VMEM((heads, group_columns, width), jnp.bfloat16),
            pltpu.VMEM(residual.shape, jnp.bfloat16),
            pltpu.VMEM((rows, width), jnp.float32),
            pltpu.VMEM((rows, width), out_type),
            pltpu.VMEM((rows, group_columns), jnp.bfloat16),
            pltpu.SemaphoreType.DMA((chunks,)),
            pltpu.SemaphoreType.DMA((heads,)),
            pltpu.SemaphoreType.DMA((heads,)),
            pltpu.SemaphoreType.DMA,
            pltpu.SemaphoreType.DMA,
            pltpu.SemaphoreType.DMA((4, chunks)),
            pltpu.SemaphoreType.DMA((4, chunks)),
        ],
        compiler_params=pltpu.CompilerParams(
            collective_id=0, has_side_effects=True, vmem_limit_bytes=60 * 1024 * 1024
        ),
    )(queries, keys, values, residual, out_weight)
    if with_residual:
        return result
    summed = lax.psum_scatter(result, "hid", scatter_dimension=1, tiled=True)
    return (residual.astype(jnp.float32) + summed).astype(jnp.bfloat16)


def solution(mesh):
    return jax.shard_map(
        functools.partial(on_device, mesh.shape["ctx"], mesh.shape["hid"]),
        mesh=mesh,
        in_specs=(
            P("ctx", "hid"),
            P("ctx", "hid"),
            P("ctx", "hid"),
            P("ctx", "hid"),
            P("hid", None),
        ),
        out_specs=P("ctx", "hid"),
        check_vma=False,
    )
```

time: 161 us -> 56.7 us (0.35)
  the two profiles are of different devices: /device:TPU:15 before, /device:TPU:8 now
where the time goes in v1:
time: 56.7 us; the launch traced here: 56.6 us
  Pallas kernels  53.4 us (94%)
  local copies, waits for them, and re-layouts  3.13 us (6%)
    pallas_call x1, Pallas kernels, on_device(): pl.pallas_call(functools.partial(block_kernel, n, with_residual), out_sha...  53.4 us
    unnamed x1, local copies, waits for them, and re-layouts  3.13 us

profile of v1, /device:TPU:8, one launch (start us, length us, event | category | flops | bytes accessed | tf_op | source)
XLA Modules:
  0.0 56.6 jit_solution(13498814805017976650)
XLA Ops:
  0.0 53.4 %shard_map.55 = bf16[256,4096]{1,0:T(8,128)(2,1)} custom-call(bf16[256,4096]{1,0:T(8,128)(2,1)} %q_hbm.1, bf16[256,1024]{1,0:T(8,128)(2,1)} %k_hbm.1, bf16[256,1024]{1,0:T(8,128)(2,1)} %v_hbm.1, bf16[256,4096]{1,0:T(8,128)(2,1)} %res_hbm.1, bf16[4096,4096]{1,0:T(8,128)(2,1)} %w_hbm.1), custom_call_target="tpu_custom_call" | custom-call | tf_op jit(solution)/shard_map/pallas_call | solution.py:244
  53.4 3.1 %copy.7 = bf16[256,4096]{1,0:T(8,128)(2,1)} copy(bf16[256,4096]{1,0:T(8,128)(2,1)} %shard_map.55) | data formatting | bytes 4194304

commit v2 on v1

--- a/solution.py
+++ b/solution.py
@@ -23,19 +23,17 @@
     v_hbm,
     res_hbm,
     w_hbm,
-    out_hbm,
+    out_ref,
     kv,
     q_vm,
     w_vm,
     res_vm,
     acc,
-    out_vm,
     att,
     own_sem,
     q_sem,
     w_sem,
     res_sem,
-    out_sem,
     send_sem,
     recv_sem,
 ):
@@ -69,14 +67,6 @@
 
     for c in range(chunks):
         own_copy(c).start()
-    for h in range(heads):
-        q_copy(h).start()
-    if with_residual:
-        res_copy = pltpu.make_async_copy(res_hbm, res_vm, res_sem)
-        res_copy.start()
-    for h in range(heads):
-        w_copy(h).start()
-
     def bit(distance):
         return (me // distance) % 2
 
@@ -116,6 +106,12 @@
             def _():
                 target = me + 8 if distance == 8 else partner(distance)
                 send(c, distance, 0, target).start()
+
+    if with_residual:
+        res_copy = pltpu.make_async_copy(res_hbm, res_vm, res_sem)
+        res_copy.start()
+    for h in range(heads):
+        q_copy(h).start()
 
     for distance in DISTANCES:
         @pl.when(me < distance)
@@ -196,6 +192,10 @@
         h = i - lead
         turn(2 * i)
 
+        @pl.when(i < heads)
+        def _():
+            w_copy(i).start()
+
         @pl.when(h >= 0)
         def _():
             q_copy(h).wait()
@@ -215,9 +215,7 @@
                     preferred_element_type=jnp.float32,
                 )
 
-    out_vm[...] = acc[...].astype(out_vm.dtype)
-    out_copy = pltpu.make_async_copy(out_vm, out_hbm, out_sem)
-    out_copy.start()
+    out_ref[...] = acc[...].astype(out_ref.dtype)
 
     for distance in DISTANCES:
         sent = sends_own(distance)
@@ -229,8 +227,6 @@
             @pl.loop(0, chunks)
             def _(c):
                 send(c, distance, 0, me).wait_send()
-
-    out_copy.wait()
 
 
 def on_device(n, hid, queries, keys, values, residual, out_weight):
@@ -243,27 +239,25 @@
     out_type = jnp.bfloat16 if with_residual else jnp.float32
     result = pl.pallas_call(
         functools.partial(block_kernel, n, with_residual),
-        out_shape=jax.ShapeDtypeStruct((rows, width), out_type),
+        out_shape=pltpu.VMEM((rows, width), out_type),
         in_specs=[pl.BlockSpec(memory_space=pl.ANY)] * 5,
-        out_specs=pl.BlockSpec(memory_space=pl.ANY),
+        out_specs=pl.BlockSpec(memory_space=pltpu.VMEM),
         scratch_shapes=[
             pltpu.VMEM((chunks, 5 * rows, HEAD_SIZE), jnp.bfloat16),
             pltpu.VMEM((heads, rows, group_columns), jnp.bfloat16),
             pltpu.VMEM((heads, group_columns, width), jnp.bfloat16),
             pltpu.VMEM(residual.shape, jnp.bfloat16),
             pltpu.VMEM((rows, width), jnp.float32),
-            pltpu.VMEM((rows, width), out_type),
             pltpu.VMEM((rows, group_columns), jnp.bfloat16),
             pltpu.SemaphoreType.DMA((chunks,)),
             pltpu.SemaphoreType.DMA((heads,)),
             pltpu.SemaphoreType.DMA((heads,)),
             pltpu.SemaphoreType.DMA,
-            pltpu.SemaphoreType.DMA,
             pltpu.SemaphoreType.DMA((4, chunks)),
             pltpu.SemaphoreType.DMA((4, chunks)),
         ],
         compiler_params=pltpu.CompilerParams(
-            collective_id=0, has_side_effects=True, vmem_limit_bytes=60 * 1024 * 1024
+            collective_id=0, has_side_effects=True, vmem_limit_bytes=54 * 1024 * 1024
         ),
     )(queries, keys, values, residual, out_weight)
     if with_residual:

time: 56.7 us -> 49.9 us (0.88)
  Pallas kernels: 53.4 us -> 48.4 us
  local copies, waits for them, and re-layouts: 3.13 us -> 1.32 us
    pallas_call x1, Pallas kernels: 53.4 us -> 48.4 us  [on_device(): pl.pallas_call(functools.partial(block_kernel, n, with_residual), out_sha...]
    unnamed x1, local copies, waits for them, and re-layouts: 3.13 us -> 1.32 us
where the time goes in v2:
time: 49.9 us; the launch traced here: 49.8 us
  Pallas kernels  48.4 us (97%)
  local copies, waits for them, and re-layouts  1.32 us (3%)
    pallas_call x1, Pallas kernels, on_device(): pl.pallas_call(functools.partial(block_kernel, n, with_residual), out_sha...  48.4 us
    unnamed x1, local copies, waits for them, and re-layouts  1.32 us

profile of v2, /device:TPU:8, one launch (start us, length us, event | category | flops | bytes accessed | tf_op | source)
XLA Modules:
  0.0 49.8 jit_solution(11641071995510626933)
XLA Ops:
  0.0 48.4 %shard_map.55 = bf16[256,4096]{1,0:T(8,128)(2,1)S(1)} custom-call(bf16[256,4096]{1,0:T(8,128)(2,1)} %q_hbm.1, bf16[256,1024]{1,0:T(8,128)(2,1)} %k_hbm.1, bf16[256,1024]{1,0:T(8,128)(2,1)} %v_hbm.1, bf16[256,4096]{1,0:T(8,128)(2,1)} %res_hbm.1, bf16[4096,4096]{1,0:T(8,128)(2,1)} %w_hbm.1), custom_call_target="tpu_custom_call" | custom-call | tf_op jit(solution)/shard_map/pallas_call | solution.py:240
  48.4 1.3 %copy.7 = bf16[256,4096]{1,0:T(8,128)(2,1)} copy(bf16[256,4096]{1,0:T(8,128)(2,1)S(1)} %shard_map.55) | data formatting | bytes 4194304
